TPU v7x, 32 devices: a whole 2x2x4 slice. The times are simulated.
32 devices in a mesh: dp: 8 (over z, x), width: 2 (over y), grid: 2 (over core).
Axes of the slice: x: 2, y: 2, z: 4, core: 2. Of those that a mesh axis runs over, the one named last changes fastest.
Arguments:
- train_acts: bfloat16 [6144, 16384], P(('dp', 'grid'), 'width'), may hold values from -6 to 6
- train_grads: bfloat16 [6144, 16384], P(('dp', 'grid'), 'width'), may hold values from -6 to 6
- query_acts: bfloat16 [512, 16384], P('dp', 'width'), may hold values from -6 to 6
- query_grads: bfloat16 [512, 16384], P('dp', 'width'), may hold values from -6 to 6
- act_inverse: bfloat16 [16384, 16384], P(('dp', 'grid'), 'width'), may hold values from -0.046875 to 0.046875
- grad_inverse: bfloat16 [16384, 16384], P(('dp', 'grid'), 'width'), may hold values from -0.046875 to 0.046875
- query_slot: int32 [16], replicated, may hold values from 0 to 15, each once
- resident: int32 [6144], P(('dp', 'grid')), may hold values 0 or 1
Outputs:
- scores: float32 [6144, 16], P(('dp', 'grid'), 'width')
All inputs are finite; a program needn't handle non-finite values. No bound on the sum of `resident` on one device may be relied on, other than what follows from the above.
Results may differ from a plain program's by a relative error of at most 0.0041.
Values may be sent and summed in bfloat16 or wider, within the bound.
A program may use at most 128 MiB of HBM per device.

v0:
```python
import math

import jax
import jax.numpy as jnp
from jax import lax
from jax.sharding import PartitionSpec as P

D = 16384
QUERIES = 16
QTOK = 32


def reorder(rows, source):
    return rows.reshape(QUERIES, QTOK, rows.shape[-1])[source].reshape(
        QUERIES * QTOK, rows.shape[-1]
    )


def precondition(inverse, rows):
    return lax.dot_general(
        inverse, rows, (((1,), (1,)), ((), ())), preferred_element_type=jnp.float32
    )


def local(
    train_acts,
    train_grads,
    query_acts,
    query_grads,
    act_inverse,
    grad_inverse,
    query_slot,
    resident,
):
    rows_acts, rows_grads = (
        lax.all_gather(query_acts, "dp", axis=0, tiled=True),
        lax.all_gather(query_grads, "dp", axis=0, tiled=True),
    )
    slots = jnp.arange(QUERIES, dtype=jnp.int32)
    source = jnp.sum(jnp.where(query_slot[:, None] == slots[None, :], slots[:, None], 0), axis=0)
    act_part = precondition(act_inverse, reorder(rows_acts, source))
    grad_part = precondition(grad_inverse, reorder(rows_grads, source))
    act_sum, grad_sum = (
        lax.psum_scatter(act_part, "width", scatter_dimension=1, tiled=True),
        lax.psum_scatter(grad_part, "width", scatter_dimension=1, tiled=True),
    )
    act_cols, grad_cols = (
        lax.all_gather(act_sum.astype(jnp.bfloat16), ("dp", "grid"), axis=0, tiled=True),
        lax.all_gather(grad_sum.astype(jnp.bfloat16), ("dp", "grid"), axis=0, tiled=True),
    )
    act_factor, grad_factor = (
        lax.all_to_all(act_cols, "width", split_axis=0, concat_axis=1, tiled=True),
        lax.all_to_all(grad_cols, "width", split_axis=0, concat_axis=1, tiled=True),
    )
    act_proj = jnp.dot(train_acts, act_factor, preferred_element_type=jnp.float32)
    grad_proj = jnp.dot(train_grads, grad_factor, preferred_element_type=jnp.float32)
    factor_scale = 1.0 / (D * math.sqrt(QTOK))
    act_share, grad_share = (
        lax.psum_scatter(act_proj, "width", scatter_dimension=1, tiled=True),
        lax.psum_scatter(grad_proj, "width", scatter_dimension=1, tiled=True),
    )
    influence = (
        jnp.sum((act_share * grad_share).reshape(act_share.shape[0], -1, QTOK), axis=2)
        * factor_scale
    )
    return influence * resident[:, None].astype(jnp.float32)


def solution(mesh):
    return jax.shard_map(
        local,
        mesh=mesh,
        in_specs=(
            P(("dp", "grid"), "width"),
            P(("dp", "grid"), "width"),
            P("dp", "width"),
            P("dp", "width"),
            P(("dp", "grid"), "width"),
            P(("dp", "grid"), "width"),
            P(),
            P(("dp", "grid")),
        ),
        out_specs=P(("dp", "grid"), "width"),
        check_vma=False,
    )
```

profile of v0, /device:TPU:0, one launch (start us, length us, event | category | flops | bytes accessed | tf_op | source)
XLA Modules:
  0.0 655.5 jit_solution(370245278560753830)
XLA Ops:
  6.5 0.0 all-gather.9.cloned.1.call-start
  6.5 0.7 all-gather.9.cloned.1.call-update
  7.3 0.0 all-gather.5.cloned.1.call-start
  7.3 0.7 all-gather.5.cloned.1.call-update
  8.0 0.0 reduce-scatter.9.cloned.1.call-start
  8.1 0.7 select_reduce_fusion
  8.8 128.3 %all-gather.9.cloned.1.call-done = bf16[512,8192]{1,0:T(8,128)(2,1)} async-done(((bf16[64,8192]{1,0:T(8,128)(2,1)}), bf16[512,8192]{1,0:T(8,128)(2,1)}) %all-gather.9.cloned.1.call-update) | async-done | bytes 8388624 | tf_op jit(solution)/shard_map/all_gather | solution.py:37
  137.1 8.3 %gather_fusion.1 = bf16[16,32,8192]{2,1,0:T(8,128)(2,1)} fusion(bf16[16,32,8192]{2,1,0:T(8,128)(2,1)} %bitcast.43, s32[1024]{0:T(1024)S(1)} %pad_clamp_fusion), kind=kCustom, calls=%fused_computation.1 | custom fusion | bytes 16777280 | tf_op jit(solution)/shard_map/gather | solution.py:14
  145.4 16.4 %convolution_bitcast_fusion = f32[1024,512]{0,1:T(8,128)} fusion(bf16[512,8192]{1,0:T(8,128)(2,1)} %bitcast.45, bf16[1024,8192]{1,0:T(8,128)(2,1)} %param.13), kind=kOutput, calls=%fused_computation.4 | convolution fusion | flops 8589934592 | bytes 27262976 | tf_op jit(solution)/shard_map/dot_general | solution.py:20
  161.8 0.0 reduce-scatter.9.cloned.1.call-update
  161.8 0.0 reduce-scatter.5.cloned.1.call-start
  161.9 100.5 %all-gather.5.cloned.1.call-done = bf16[512,8192]{1,0:T(8,128)(2,1)} async-done(((bf16[64,8192]{1,0:T(8,128)(2,1)}), bf16[512,8192]{1,0:T(8,128)(2,1)}) %all-gather.5.cloned.1.call-update) | async-done | bytes 8388624 | tf_op jit(solution)/shard_map/all_gather | solution.py:36
  262.4 8.3 %gather_fusion = bf16[16,32,8192]{2,1,0:T(8,128)(2,1)} fusion(bf16[16,32,8192]{2,1,0:T(8,128)(2,1)} %bitcast.42, s32[1024]{0:T(1024)S(1)} %pad_clamp_fusion), kind=kCustom, calls=%fused_computation | custom fusion | bytes 16777280 | tf_op jit(solution)/shard_map/gather | solution.py:14
  270.7 15.8 %convolution_bitcast_fusion.1 = f32[1024,512]{0,1:T(8,128)} fusion(bf16[512,8192]{1,0:T(8,128)(2,1)} %bitcast.44, bf16[1024,8192]{1,0:T(8,128)(2,1)} %param.12), kind=kOutput, calls=%fused_computation.5 | convolution fusion | flops 8589934592 | bytes 27262976 | tf_op jit(solution)/shard_map/dot_general | solution.py:20
  286.5 0.0 reduce-scatter.5.cloned.1.call-update
  286.5 0.0 all-gather.11.cloned.1.call-start
  286.6 8.1 %reduce-scatter.9.cloned.1.call-done = f32[1024,256]{0,1:T(8,128)} async-done(((f32[1024,512]{0,1:T(8,128)}), f32[1024,256]{0,1:T(8,128)}) %reduce-scatter.9.cloned.1.call-update) | async-done | bytes 1048592 | tf_op jit(solution)/shard_map/reduce_scatter | solution.py:45
  294.7 2.1 convert_element_type.11
  296.8 0.0 all-gather.11.cloned.1.call-update
  296.8 0.0 all-gather.7.cloned.1.call-start
  296.9 31.9 %reduce-scatter.5.cloned.1.call-done = f32[1024,256]{0,1:T(8,128)} async-done(((f32[1024,512]{0,1:T(8,128)}), f32[1024,256]{0,1:T(8,128)}) %reduce-scatter.5.cloned.1.call-update) | async-done | bytes 1048592 | tf_op jit(solution)/shard_map/reduce_scatter | solution.py:44
  328.8 2.1 convert_element_type.10
  330.9 0.0 all-gather.7.cloned.1.call-update
  330.9 74.9 %all-gather.11.cloned.1.call-done = bf16[16384,256]{0,1:T(8,128)(2,1)} async-done(((bf16[1024,256]{0,1:T(8,128)(2,1)}), bf16[16384,256]{0,1:T(8,128)(2,1)}) %all-gather.11.cloned.1.call-update) | async-done | bytes 8388624 | tf_op jit(solution)/shard_map/all_gather | solution.py:49
  405.8 7.6 %copy.17 = bf16[32,2,8,8192]{3,2,0,1:T(8,128)(2,1)} copy(bf16[32,2,8,8192]{3,2,1,0:T(8,128)(2,1)} %bitcast.46) | data formatting | bytes 16777216 | tf_op jit(solution)/shard_map/all_to_all | solution.py:53
  413.4 7.0 %all-to-all-start.1 = ((bf16[2,8192,256]{1,2,0:T(8,128)(2,1)}), bf16[2,8192,256]{1,2,0:T(8,128)(2,1)}, u32[]{:S(2)}, u32[]{:S(2)}) async-start(bf16[2,8192,256]{1,2,0:T(8,128)(2,1)} %bitcast.41), calls=%async_computation.4 | async-start | bytes 16777216 | tf_op jit(solution)/shard_map/all_to_all | solution.py:53
  420.3 60.7 %all-gather.7.cloned.1.call-done = bf16[16384,256]{0,1:T(8,128)(2,1)} async-done(((bf16[1024,256]{0,1:T(8,128)(2,1)}), bf16[16384,256]{0,1:T(8,128)(2,1)}) %all-gather.7.cloned.1.call-update) | async-done | bytes 8388624 | tf_op jit(solution)/shard_map/all_gather | solution.py:48
  481.0 7.6 %copy.18 = bf16[32,2,8,8192]{3,2,0,1:T(8,128)(2,1)} copy(bf16[32,2,8,8192]{3,2,1,0:T(8,128)(2,1)} %bitcast.47) | data formatting | bytes 16777216 | tf_op jit(solution)/shard_map/all_to_all | solution.py:52
  488.6 24.8 %all-to-all-done.1 = bf16[2,8192,256]{1,2,0:T(8,128)(2,1)} async-done(((bf16[2,8192,256]{1,2,0:T(8,128)(2,1)}), bf16[2,8192,256]{1,2,0:T(8,128)(2,1)}, u32[]{:S(2)}, u32[]{:S(2)}) %all-to-all-start.1) | async-done | bytes 8388640 | tf_op jit(solution)/shard_map/all_to_all | solution.py:53
  513.3 7.0 %all-to-all-start = ((bf16[2,8192,256]{1,2,0:T(8,128)(2,1)}), bf16[2,8192,256]{1,2,0:T(8,128)(2,1)}, u32[]{:S(2)}, u32[]{:S(2)}) async-start(bf16[2,8192,256]{1,2,0:T(8,128)(2,1)} %bitcast.40), calls=%async_computation.1 | async-start | bytes 16777216 | tf_op jit(solution)/shard_map/all_to_all | solution.py:52
  520.3 0.2 reduce-scatter.11.cloned.1.call-start
  520.5 10.6 %convolution_bitcast_fusion.2 = f32[384,512]{0,1:T(8,128)} fusion(bf16[8192,512]{0,1:T(8,128)(2,1)} %bitcast.12, bf16[384,8192]{1,0:T(8,128)(2,1)} %param.9), kind=kOutput, calls=%fused_computation.6 | convolution fusion | flops 3221225472 | bytes 15466496 | tf_op jit(solution)/shard_map/dot_general | solution.py:56
  531.2 0.0 reduce-scatter.11.cloned.1.call-update
  531.2 0.0 reduce-scatter.7.cloned.1.call-start
  531.2 89.7 %all-to-all-done = bf16[2,8192,256]{1,2,0:T(8,128)(2,1)} async-done(((bf16[2,8192,256]{1,2,0:T(8,128)(2,1)}), bf16[2,8192,256]{1,2,0:T(8,128)(2,1)}, u32[]{:S(2)}, u32[]{:S(2)}) %all-to-all-start) | async-done | bytes 8388640 | tf_op jit(solution)/shard_map/all_to_all | solution.py:52
  621.0 0.0 copy-start
  621.0 10.6 %convolution_bitcast_fusion.3 = f32[384,512]{0,1:T(8,128)} fusion(bf16[8192,512]{0,1:T(8,128)(2,1)} %bitcast.6, bf16[384,8192]{1,0:T(8,128)(2,1)} %param.8), kind=kOutput, calls=%fused_computation.7 | convolution fusion | flops 3221225472 | bytes 15466496 | tf_op jit(solution)/shard_map/dot_general | solution.py:55
  631.5 0.0 reduce-scatter.7.cloned.1.call-update
  631.6 0.0 copy-done
  631.6 0.0 reduce-scatter.11.cloned.1.call-done
  631.6 15.2 %reduce-scatter.7.cloned.1.call-done = f32[384,256]{0,1:T(8,128)} async-done(((f32[384,512]{0,1:T(8,128)}), f32[384,256]{0,1:T(8,128)}) %reduce-scatter.7.cloned.1.call-update) | async-done | bytes 393232 | tf_op jit(solution)/shard_map/reduce_scatter | solution.py:59
  646.8 1.2 bitcast_reduce_fusion
  648.0 0.6 broadcast_multiply_fusion
  (3 shorter events, 0.0 us)
Async XLA Ops:
  6.5 130.6 %all-gather.9.cloned.1.call-start = ((), (), s32[]{:S(2)}) async-start(), calls=%async_computation.10 | async-start | bytes 9437184 | tf_op jit(solution)/shard_map/all_gather | solution.py:37
  7.3 255.2 %all-gather.5.cloned.1.call-start = ((), (), s32[]{:S(2)}) async-start(), calls=%async_computation.6 | async-start | bytes 9437184 | tf_op jit(solution)/shard_map/all_gather | solution.py:36
  8.0 286.7 %reduce-scatter.9.cloned.1.call-start = ((), (), s32[]{:S(2)}) async-start(), calls=%async_computation.11 | async-start | bytes 3145728 | tf_op jit(solution)/shard_map/reduce_scatter | solution.py:45
  161.8 166.9 %reduce-scatter.5.cloned.1.call-start = ((), (), s32[]{:S(2)}) async-start(), calls=%async_computation.7 | async-start | bytes 3145728 | tf_op jit(solution)/shard_map/reduce_scatter | solution.py:44
  286.5 119.2 %all-gather.11.cloned.1.call-start = ((), (), s32[]{:S(2)}) async-start(), calls=%async_computation.12 | async-start | bytes 8912896 | tf_op jit(solution)/shard_map/all_gather | solution.py:49
  296.8 184.1 %all-gather.7.cloned.1.call-start = ((), (), s32[]{:S(2)}) async-start(), calls=%async_computation.8 | async-start | bytes 8912896 | tf_op jit(solution)/shard_map/all_gather | solution.py:48
  413.4 100.0 %all-to-all-start.1 = ((bf16[2,8192,256]{1,2,0:T(8,128)(2,1)}), bf16[2,8192,256]{1,2,0:T(8,128)(2,1)}, u32[]{:S(2)}, u32[]{:S(2)}) async-start(bf16[2,8192,256]{1,2,0:T(8,128)(2,1)} %bitcast.41), calls=%async_computation.4 | async-start | bytes 16777216 | tf_op jit(solution)/shard_map/all_to_all | solution.py:53
  513.3 107.6 %all-to-all-start = ((bf16[2,8192,256]{1,2,0:T(8,128)(2,1)}), bf16[2,8192,256]{1,2,0:T(8,128)(2,1)}, u32[]{:S(2)}, u32[]{:S(2)}) async-start(bf16[2,8192,256]{1,2,0:T(8,128)(2,1)} %bitcast.40), calls=%async_computation.1 | async-start | bytes 16777216 | tf_op jit(solution)/shard_map/all_to_all | solution.py:52
  520.3 111.3 %reduce-scatter.11.cloned.1.call-start = ((), (), s32[]{:S(2)}) async-start(), calls=%async_computation.13 | async-start | bytes 1179648 | tf_op jit(solution)/shard_map/reduce_scatter | solution.py:60
  531.2 115.6 %reduce-scatter.7.cloned.1.call-start = ((), (), s32[]{:S(2)}) async-start(), calls=%async_computation.9 | async-start | bytes 1179648 | tf_op jit(solution)/shard_map/reduce_scatter | solution.py:59
  621.0 10.6 %copy-start = (s32[384]{0:T(512)S(1)}, s32[384]{0:T(512)}, u32[]{:S(2)}) copy-start(s32[384]{0:T(512)} %param.15) | copy-start | bytes 4612
Sparse Core Ops, SparseCore 0:
  9.5 127.6 all-gather.8
  139.3 123.1 all-gather.4
  264.7 30.0 reduce-scatter.8
  296.9 31.8 reduce-scatter.4
  330.8 74.9 all-gather.10
  407.8 73.1 all-gather.6
  531.3 24.8 reduce-scatter.10
  631.7 15.1 reduce-scatter.6
where the time goes:
time: 656 us; the launch traced here: 655 us
  waiting for transfers between devices  536 us (82%)
  matrix products  53.4 us (8%)
  local copies, waits for them, and re-layouts  31.7 us (5%)
  starting transfers between devices  14.4 us (2%)
  between operations  13.6 us (2%)
  other arithmetic  6.74 us (1%)
    all_gather x1, waiting for transfers between devices, local(): lax.all_gather(query_grads, 'dp', axis=0, tiled=True)  128 us
    all_gather x1, waiting for transfers between devices, local(): lax.all_gather(query_acts, 'dp', axis=0, tiled=True)  101 us
    all_to_all x1, waiting for transfers between devices, local(): lax.all_to_all(act_cols, 'width', split_axis=0, concat_axis=1, tiled=True)  89.7 us
    all_gather x1, waiting for transfers between devices, local(): lax.all_gather(grad_sum.astype(jnp.bfloat16), ('dp', 'grid'), axis=0, til...  74.9 us
    all_gather x1, waiting for transfers between devices, local(): lax.all_gather(act_sum.astype(jnp.bfloat16), ('dp', 'grid'), axis=0, tile...  60.7 us
    dot_general x2, matrix products, precondition(): lax.dot_general(inverse, rows, (((1,), (1,)), ((), ())), preferred_elemen...  32.2 us
    reduce_scatter x1, waiting for transfers between devices, local(): lax.psum_scatter(act_part, 'width', scatter_dimension=1, tiled=True)  31.9 us
    all_to_all x1, waiting for transfers between devices, local(): lax.all_to_all(grad_cols, 'width', split_axis=0, concat_axis=1, tiled=True)  24.8 us
  transfers between devices with their start and end apart: 10, of which 9 were waited for; matrix products, arithmetic and copies ran while one was open for 14% of the time, Pallas kernels for 0%

commit v1 on v0

v1 whole, which is shorter than its diff:
```python
import functools
import math

import jax
import jax.numpy as jnp
from jax import lax
from jax.experimental import pallas as pl
from jax.experimental.pallas import tpu as pltpu
from jax.sharding import PartitionSpec as P

LANES = 2
CUTS = 2
PARTS = 2
BLOCKS = 4
VMEM = 62 * 1024 * 1024


def pipeline(
    n_dp, n_width, n_grid, seg_sum,
    qa, qg, ia, ig, ta, tg, out,
    qbuf, ibuf, part, rs, mine, fac, proj, prs, infl,
    load_sem, inv_sem, train_sem,
    a_recv, a_core, a_send,
    rs_send, rs_recv, w_send, w_recv,
    c_recv, c_core, c_send,
    p_send, p_recv, f_send, f_recv,
):
    dp, w, g = lax.axis_index("dp"), lax.axis_index("width"), lax.axis_index("grid")
    line = n_dp // LANES
    z, x = dp // LANES, lax.rem(dp, LANES)
    q_hbm, inv_hbm, train_hbm = (qa, qg), (ia, ig), (ta, tg)
    q_rows = qa.shape[0]
    half = q_rows // n_grid
    feats = qa.shape[1] // CUTS
    rows = ia.shape[0]
    block = rows // BLOCKS
    cut = rows // PARTS
    tokens = ta.shape[0]
    cols = part.shape[-1]
    group = n_dp // n_width
    home = dp // group
    slot = lax.rem(dp, group)

    def device(d=None, width=None, grid=None):
        return {
            "dp": dp if d is None else d,
            "width": w if width is None else width,
            "grid": g if grid is None else grid,
        }

    def remote(src, dst, send, recv, to):
        return pltpu.make_async_remote_copy(
            src_ref=src, dst_ref=dst, send_sem=send, recv_sem=recv,
            device_id=to, device_id_type=pl.DeviceIdType.MESH,
        )

    def other(j):
        return lax.rem(w + j, n_width)

    class Gather:
        def __init__(self, ref, recv, core, send, lo, count, own_core):
            self.ref, self.recv, self.core, self.send = ref, recv, core, send
            self.lo, self.count, self.own_core = lo, count, own_core

        def copy(self, o, lane, d):
            ref = self.ref(o, lane, g)
            if d == 0:
                to = device((z + 1) * LANES + x)
            elif d == 1:
                to = device((z - 1) * LANES + x)
            elif d < 1 + LANES:
                to = device(z * LANES + lax.rem(x + d - 1, LANES))
            else:
                to = device(grid=lax.rem(g + d - LANES, n_grid))
            recv = self.recv(o, lane) if d < 1 + LANES else self.core(o, lane, g)
            return remote(ref, ref, self.send(o, lane, d), recv, to)

        def wait(self, o, lane):
            self.copy(o, lane, 2).wait_recv()

        def has(self, o):
            return (o >= self.lo) & (o < self.lo + self.count)

        def sends(self, o, lane, up, down, across, core, act):
            if up:
                pl.when(z + 1 < line)(lambda: act(self.copy(o, lane, 0)))
            if down:
                pl.when(z > 0)(lambda: act(self.copy(o, lane, 1)))
            if across:
                for d in range(2, 1 + LANES):
                    act(self.copy(o, lane, d))
            if core:
                for d in range(1 + LANES, LANES + n_grid):
                    act(self.copy(o, lane, d))

        def walk(self, act, stage, step):
            first = act is not None
            run = act if first else (lambda c: c.wait_send())
            if stage == 0:
                pl.when(self.has(z))(
                    lambda: self.sends(z, x, True, True, True, self.own_core, run))
            elif stage == 1:
                for o, up in ((z - step, True), (z + step, False)):
                    @pl.when(self.has(o))
                    def _(o=o, up=up):
                        if first:
                            self.wait(o, x)
                        self.sends(o, x, up, not up, True, True, run)
            else:
                for o in (z,) if step == 0 else (z - step, z + step):
                    @pl.when(self.has(o))
                    def _(o=o):
                        for d in range(1, LANES):
                            lane = lax.rem(x + d, LANES)
                            if first:
                                self.wait(o, lane)
                            self.sends(o, lane, False, False, False, True, run)

        def start(self):
            self.walk(lambda c: c.start(), 0, 0)

        def along(self, step):
            self.walk(lambda c: c.start(), 1, step)

        def across(self, step):
            self.walk(lambda c: c.start(), 2, step)

        def finish(self):
            for i in range(self.count):
                o = self.lo + i
                for lane in range(LANES):
                    def _(o=o, lane=lane):
                        for j in range(1, n_grid):
                            src = lax.rem(g + j, n_grid)
                            ref = self.ref(o, lane, src)
                            remote(ref, ref, self.send(o, lane, 0), self.core(o, lane, src),
                                   device(grid=src)).wait_recv()
                    if self.own_core:
                        _()
                    else:
                        pl.when((o != z) | (lane != x))(_)

        def drain(self):
            self.walk(None, 0, 0)
            for step in range(1, line):
                self.walk(None, 1, step)
            for step in range(line):
                self.walk(None, 2, step)

    def query_gather(k):
        a, f = divmod(k, CUTS)

        def ref(o, lane, gg):
            at = pl.multiple_of((o * LANES + lane) * q_rows + gg * half, half)
            return qbuf.at[a, f, pl.ds(at, half)]

        return Gather(
            ref,
            lambda o, l: a_recv.at[k, o * LANES + l],
            lambda o, l, gg: a_core.at[k, o * LANES + l, gg],
            lambda o, l, d: a_send.at[k, o * LANES + l, d],
            0, line, False)

    lines = group // LANES

    def factor_gather(a, h, j):
        c = other(j)

        def local(o, l):
            return (o - w * lines) * LANES + l

        def ref(o, lane, gg):
            return fac.at[a, c, local(o, lane), gg, pl.ds(h * cut, cut)]

        return Gather(
            ref,
            lambda o, l: c_recv.at[a, h, c, local(o, l)],
            lambda o, l, gg: c_core.at[a, h, c, local(o, l), gg],
            lambda o, l, d: c_send.at[a, h, c, local(o, l), d],
            w * lines, lines, True)

    units = 2 * CUTS * BLOCKS

    def inv_load(u):
        k, rb = divmod(u, BLOCKS)
        a, f = divmod(k, CUTS)
        s = u % ibuf.shape[0]
        return pltpu.make_async_copy(
            inv_hbm[a].at[pl.ds(rb * block, block), pl.ds(f * feats, feats)],
            ibuf.at[s], inv_sem.at[s])

    def rs_copy(a, rb, j):
        c = other(j)
        at = pl.ds(rb * block, block)
        return remote(part.at[a, c, at], rs.at[a, n_width - 1 - j, at],
                      rs_send.at[a, rb, j], rs_recv.at[a, rb, j], device(width=c))

    def multiply(u):
        k, rb = divmod(u, BLOCKS)
        a, f = divmod(k, CUTS)
        ahead = u + ibuf.shape[0] - 1
        if ahead < units:
            inv_load(ahead).start()
        inv_load(u).wait()
        at = pl.ds(rb * block, block)
        left = ibuf[u % ibuf.shape[0]]
        wide = max(cols, min(256, cols * n_width))
        per = wide // cols
        for n in range(cols * n_width // wide):
            prod = lax.dot_general(
                left, qbuf[a, f, n * wide:(n + 1) * wide], (((1,), (1,)), ((), ())),
                preferred_element_type=jnp.float32)
            for i in range(per):
                piece = prod[:, i * cols:(i + 1) * cols]
                if f == 0:
                    part[a, n * per + i, at] = piece
                else:
                    part[a, n * per + i, at] += piece
        if f == CUTS - 1:
            for j in range(1, n_width):
                rs_copy(a, rb, j).start()

    def hand_copy(a, h, src_w, j):
        at = pl.ds(h * cut, cut)
        return remote(mine.at[a, at], fac.at[a, src_w, slot, g, at],
                      w_send.at[a, h], w_recv.at[a, h, j], device(width=home))

    def total(a, h):
        per = BLOCKS // PARTS
        for rb in range(h * per, (h + 1) * per):
            at = pl.ds(rb * block, block)
            for j in range(1, n_width):
                rs_copy(a, rb, j).wait_recv()
            value = part[a, w, at]
            for j in range(1, n_width):
                value = value + rs[a, n_width - 1 - j, at]
            value = value.astype(jnp.bfloat16)

            @pl.when(w == home)
            def _():
                fac[a, w, slot, g, at] = value

            @pl.when(w != home)
            def _():
                mine[a, at] = value

        @pl.when(w != home)
        def _():
            hand_copy(a, h, w, lax.rem(home - w + n_width, n_width)).start()

    def handed(a, h, j):
        if j > 0:
            @pl.when(w == home)
            def _():
                hand_copy(a, h, other(j), n_width - j).wait_recv()

    def train_load(a, f):
        return pltpu.make_async_copy(
            train_hbm[a].at[:, pl.ds(f * feats, feats)],
            qbuf.at[a, f, pl.ds(0, tokens)], train_sem.at[a, f])

    def project(a, h, c):
        acc = None
        for b in range(group * n_grid):
            at = b * rows + h * cut
            f, col = divmod(at, feats)
            term = jnp.dot(
                qbuf[a, f, 0:tokens, col:col + cut],
                fac[a, c, b // n_grid, b % n_grid, pl.ds(h * cut, cut)],
                preferred_element_type=jnp.float32)
            acc = term if acc is None else acc + term
        if h == 0:
            proj[a, c] = acc
        else:
            proj[a, c] += acc

    def p_copy(a, j):
        c = other(j)
        return remote(proj.at[a, c], prs.at[a, n_width - 1 - j],
                      p_send.at[a, j], p_recv.at[a, j], device(width=c))

    def f_copy(j):
        return remote(infl.at[w], infl.at[w], f_send.at[j], f_recv.at[j],
                      device(width=other(j)))

    own = pl.ds(pl.multiple_of(dp * q_rows, q_rows), q_rows)
    loads = []
    for a in range(2):
        for f in range(CUTS):
            loads.append(pltpu.make_async_copy(
                q_hbm[a].at[:, pl.ds(f * feats, feats)], qbuf.at[a, f, own],
                load_sem.at[a, f]))
            loads[-1].start()
    for u in range(ibuf.shape[0] - 1):
        inv_load(u).start()

    barrier = pltpu.get_barrier_semaphore()

    def hello(to):
        pl.semaphore_signal(barrier, inc=1, device_id=to, device_id_type=pl.DeviceIdType.MESH)

    pl.when(z + 1 < line)(lambda: hello(device((z + 1) * LANES + x)))
    pl.when(z > 0)(lambda: hello(device((z - 1) * LANES + x)))
    for j in range(1, LANES):
        hello(device(z * LANES + lax.rem(x + j, LANES)))
    for j in range(1, n_grid):
        hello(device(grid=lax.rem(g + j, n_grid)))
    for j in range(1, n_width):
        hello(device(width=other(j)))
    ends = jnp.where(z + 1 < line, 1, 0) + jnp.where(z > 0, 1, 0)
    pl.semaphore_wait(barrier, ends + (LANES - 1 + n_grid - 1 + n_width - 1))

    for load in loads:
        load.wait()

    chunks = [query_gather(k) for k in range(2 * CUTS)]
    factors = [[[factor_gather(a, h, j) for j in range(n_width)] for h in range(PARTS)]
               for a in range(2)]

    def run(todo, count):
        for _ in range(min(count, len(todo))):
            todo.pop(0)()

    def begin(a, h):
        for j in range(n_width):
            handed(a, h, j)
            factors[a][h][j].start()

    chunks[0].start()
    for k in range(2 * CUTS):
        chunk = chunks[k]
        todo = []
        if k > 0:
            todo = [functools.partial(multiply, (k - 1) * BLOCKS + b) for b in range(BLOCKS)]
        for step in range(1, line):
            chunk.along(step)
            run(todo, 1)
            if step == line - 1 and k + 1 < 2 * CUTS:
                chunks[k + 1].start()
            chunk.across(step - 1)
        run(todo, len(todo))
        if k == 2 * CUTS - 1:
            for h in range(PARTS):
                total(0, h)
            for h in range(PARTS):
                begin(0, h)
        chunk.across(line - 1)
        chunk.finish()

    def spread(a, todo):
        for h in range(PARTS):
            for step in range(1, line):
                for one in factors[a][h]:
                    one.along(step)
                run(todo, 1)
                for one in factors[a][h]:
                    one.across(step - 1)
            for one in factors[a][h]:
                one.across(line - 1)

    for f in range(CUTS):
        chunks[f].drain()
        train_load(0, f).start()
    todo = [functools.partial(multiply, (2 * CUTS - 1) * BLOCKS + b) for b in range(BLOCKS)]

    def second():
        for f in range(CUTS):
            chunks[CUTS + f].drain()
            train_load(1, f).start()

    todo.append(second)
    spread(0, todo)
    run(todo, len(todo))
    for h in range(PARTS):
        total(1, h)
    for h in range(PARTS):
        begin(1, h)
    for f in range(CUTS):
        train_load(0, f).wait()

    def first_proj(h):
        for one in factors[0][h]:
            one.finish()
        for c in range(n_width):
            project(0, h, c)

    def first_sends():
        for j in range(1, n_width):
            p_copy(0, j).start()

    todo = [functools.partial(first_proj, h) for h in range(PARTS)] + [first_sends]
    spread(1, todo)
    run(todo, len(todo))
    for f in range(CUTS):
        train_load(1, f).wait()
    for h in range(PARTS):
        for one in factors[1][h]:
            one.finish()
        for c in range(n_width):
            project(1, h, c)
    for j in range(1, n_width):
        p_copy(1, j).start()
    shares = []
    for a in range(2):
        for j in range(1, n_width):
            p_copy(a, j).wait_recv()
        value = proj[a, w]
        for j in range(1, n_width):
            value = value + prs[a, n_width - 1 - j]
        shares.append(value)
    per_seq = seg_sum[1]
    shape = (infl.shape[1], cols)
    pick = (lax.broadcasted_iota(jnp.int32, shape, 1) // per_seq
            == lax.broadcasted_iota(jnp.int32, shape, 0)).astype(jnp.float32)
    infl[w] = lax.dot_general(
        pick, shares[0] * shares[1], (((1,), (1,)), ((), ())),
        precision=lax.Precision.HIGHEST, preferred_element_type=jnp.float32) * seg_sum[0]
    for j in range(1, n_width):
        f_copy(j).start()

    for j in range(1, n_width):
        src = other(j)
        remote(infl.at[src], infl.at[src], f_send.at[j], f_recv.at[n_width - j],
               device(width=src)).wait_recv()
    out[...] = infl[...]
    for a in range(2):
        for h in range(PARTS):
            for one in factors[a][h]:
                one.drain()
            pl.when(w != home)(lambda a=a, h=h: hand_copy(a, h, w, 0).wait_send())
        for rb in range(BLOCKS):
            for j in range(1, n_width):
                rs_copy(a, rb, j).wait_send()
        for j in range(1, n_width):
            p_copy(a, j).wait_send()
    for j in range(1, n_width):
        f_copy(j).wait_send()


def solution(mesh):
    n_dp, n_width, n_grid = (mesh.shape[n] for n in ("dp", "width", "grid"))

    def local(train_acts, train_grads, query_acts, query_grads, act_inverse, grad_inverse,
              query_slot, resident):
        queries = query_slot.shape[0]
        q_all = query_acts.shape[0] * n_dp
        per_seq = q_all // queries
        depth = query_acts.shape[1]
        feats = depth // CUTS
        rows = act_inverse.shape[0]
        tokens = train_acts.shape[0]
        cols = q_all // n_width
        group = n_dp // n_width
        scale = 1.0 / (depth * n_width * math.sqrt(per_seq))
        bf, f32 = jnp.bfloat16, jnp.float32
        dma = pltpu.SemaphoreType.DMA
        ways = LANES + n_grid
        hbm = pl.BlockSpec(memory_space=pl.ANY)
        flops = 4 * rows * depth * q_all + 4 * tokens * depth * q_all
        moved = 4 * (rows + tokens + q_all) * depth
        table = pl.pallas_call(
            functools.partial(pipeline, n_dp, n_width, n_grid, (scale, per_seq)),
            out_shape=jax.ShapeDtypeStruct((n_width, queries // n_width, tokens), f32),
            in_specs=[hbm] * 6,
            out_specs=pl.BlockSpec(memory_space=pltpu.VMEM),
            scratch_shapes=[
                pltpu.VMEM((2, CUTS, q_all, feats), bf),
                pltpu.VMEM((3, rows // BLOCKS, feats), bf),
                pltpu.VMEM((2, n_width, rows, cols), f32),
                pltpu.VMEM((2, n_width - 1, rows, cols), f32),
                pltpu.VMEM((2, rows, cols), bf),
                pltpu.VMEM((2, n_width, group, n_grid, rows, cols), bf),
                pltpu.VMEM((2, n_width, tokens, cols), f32),
                pltpu.VMEM((2, n_width - 1, tokens, cols), f32),
                pltpu.VMEM((n_width, queries // n_width, tokens), f32),
                dma((2, CUTS)), dma((3,)), dma((2, CUTS)),
                dma((2 * CUTS, n_dp)), dma((2 * CUTS, n_dp, n_grid)), dma((2 * CUTS, n_dp, ways)),
                dma((2, BLOCKS, n_width)), dma((2, BLOCKS, n_width)),
                dma((2, PARTS)), dma((2, PARTS, n_width)),
                dma((2, PARTS, n_width, group)), dma((2, PARTS, n_width, group, n_grid)),
                dma((2, PARTS, n_width, group, ways)),
                dma((2, n_width)), dma((2, n_width)), dma((n_width,)), dma((n_width,)),
            ],
            compiler_params=pltpu.CompilerParams(
                collective_id=0, has_side_effects=True, vmem_limit_bytes=VMEM),
            cost_estimate=pl.CostEstimate(flops=flops, bytes_accessed=moved, transcendentals=0),
        )(query_acts, query_grads, act_inverse, grad_inverse, train_acts, train_grads)
        share = queries // n_width
        slots = lax.axis_index("width") * share + jnp.arange(share, dtype=jnp.int32)
        hit = query_slot[:, None] == slots[None, :]
        picked = jnp.sum(
            jnp.where(hit[:, :, None], table.reshape(queries, 1, tokens), 0.0), axis=0)
        return picked.T * resident[:, None].astype(f32)

    return jax.shard_map(
        local,
        mesh=mesh,
        in_specs=(
            P(("dp", "grid"), "width"),
            P(("dp", "grid"), "width"),
            P("dp", "width"),
            P("dp", "width"),
            P(("dp", "grid"), "width"),
            P(("dp", "grid"), "width"),
            P(),
            P(("dp", "grid")),
        ),
        out_specs=P(("dp", "grid"), "width"),
        check_vma=False,
    )
```

time: 656 us -> 255 us (0.39)
  waiting for transfers between devices: 536 us -> 0 us
  Pallas kernels: 0 us -> 250 us
  matrix products: 53.4 us -> 0 us
  local copies, waits for them, and re-layouts: 31.7 us -> 0.01 us
  starting transfers between devices: 14.4 us -> 0 us
  between operations: 13.6 us -> 0.05 us
    all_gather x4 -> x0, waiting for transfers between devices: 364 us -> none  [the longest x1 128 us: local(): lax.all_gather(query_grads, 'dp', axis=0, tiled=True)]
    pallas_call x0 -> x1, Pallas kernels: none -> 250 us  [local(): pl.pallas_call(functools.partial(pipeline, n_dp, n_width, n_grid, (scale,...]
    all_to_all x2 -> x0, waiting for transfers between devices: 114 us -> none  [the longest x1 89.7 us: local(): lax.all_to_all(act_cols, 'width', split_axis=0, concat_axis=1, tiled=True)]
    reduce_scatter x4 -> x0, waiting for transfers between devices: 55.2 us -> none  [the longest x1 31.9 us: local(): lax.psum_scatter(act_part, 'width', scatter_dimension=1, tiled=True)]
    dot_general x4 -> x0, matrix products: 53.4 us -> none  [the longest x2 32.2 us: precondition(): lax.dot_general(inverse, rows, (((1,), (1,)), ((), ())), preferred_elemen...]
    gather x2 -> x0, local copies, waits for them, and re-layouts: 16.6 us -> none  [reorder(): rows.reshape(QUERIES, QTOK, rows.shape[-1])[source]]
    all_to_all x2 -> x0, local copies, waits for them, and re-layouts: 15.2 us -> none  [the longest x1 7.6 us: local(): lax.all_to_all(grad_cols, 'width', split_axis=0, concat_axis=1, tiled=True)]
    all_to_all x2 -> x0, starting transfers between devices: 13.9 us -> none  [the longest x1 6.96 us: local(): lax.all_to_all(act_cols, 'width', split_axis=0, concat_axis=1, tiled=True)]
  transfers between devices with their start and end apart: 10 -> 0, of which waited for: 9 -> 0; matrix products, arithmetic and copies ran while one was open for 14% -> 0% of each run, Pallas kernels for 0% -> 0%
where the time goes in v1:
time: 255 us; the launch traced here: 252 us
  Pallas kernels  250 us (98%)
    pallas_call x1, Pallas kernels, local(): pl.pallas_call(functools.partial(pipeline, n_dp, n_width, n_grid, (scale,...  250 us

profile of v1, /device:TPU:0, one launch (start us, length us, event | category | flops | bytes accessed | tf_op | source)
XLA Modules:
  0.0 251.6 jit_solution(16849958087852356634)
XLA Ops:
  0.0 0.0 copy-start.1
  0.0 0.0 copy-start
  0.0 250.0 %shard_map.82 = f32[2,8,384]{2,1,0:T(8,128)} custom-call(bf16[64,8192]{1,0:T(8,128)(2,1)} %qa.1, bf16[64,8192]{1,0:T(8,128)(2,1)} %qg.1, bf16[1024,8192]{1,0:T(8,128)(2,1)} %ia.1, bf16[1024,8192]{1,0:T(8,128)(2,1)} %ig.1, bf16[384,8192]{1,0:T(8,128)(2,1)} %ta.1, bf16[384,8192]{1,0:T(8,128)(2,1)} %tg.1), custom_call_target="tpu_custom_call" | custom-call | flops 23622320128 | bytes 62914560 | tf_op jit(solution)/shard_map/pallas_call | solution.py:461
  250.1 0.0 copy-done.1
  250.1 0.1 broadcast_compare_fusion
  250.1 0.8 select_reduce_fusion
  251.0 0.0 copy-done
  251.0 0.6 multiply_bitcast_fusion
  (2 shorter events, 0.0 us)
Async XLA Ops:
  0.0 250.1 %copy-start.1 = (s32[16]{0:T(128)S(1)}, s32[16]{0:T(128)}, u32[]{:S(2)}) copy-start(s32[16]{0:T(128)} %param.14) | copy-start | bytes 196
  0.0 251.0 %copy-start = (s32[384]{0:T(512)S(1)}, s32[384]{0:T(512)}, u32[]{:S(2)}) copy-start(s32[384]{0:T(512)} %param.15) | copy-start | bytes 4612

commit v2 on v1

--- a/solution.py
+++ b/solution.py
@@ -58,7 +58,8 @@
         return lax.rem(w + j, n_width)
 
     class Gather:
-        def __init__(self, ref, recv, core, send, lo, count, own_core):
+        def __init__(self, ref, recv, core, send, lo, count, own_core, along=-1):
+            self.through = along
             self.ref, self.recv, self.core, self.send = ref, recv, core, send
             self.lo, self.count, self.own_core = lo, count, own_core
 
@@ -105,16 +106,22 @@
                     def _(o=o, up=up):
                         if first:
                             self.wait(o, x)
-                        self.sends(o, x, up, not up, True, True, run)
+                        self.sends(o, x, up, not up, False, True, run)
+                        pl.when(o != self.through)(
+                            lambda: self.sends(o, x, False, False, True, False, run))
             else:
-                for o in (z,) if step == 0 else (z - step, z + step):
+                ways = ((z, True, True),) if step == 0 else (
+                    (z - step, True, False), (z + step, False, True))
+                for o, up, down in ways:
                     @pl.when(self.has(o))
-                    def _(o=o):
+                    def _(o=o, up=up, down=down):
                         for d in range(1, LANES):
                             lane = lax.rem(x + d, LANES)
                             if first:
                                 self.wait(o, lane)
                             self.sends(o, lane, False, False, False, True, run)
+                            pl.when(o == self.through)(
+                                lambda: self.sends(o, lane, up, down, False, False, run))
 
         def start(self):
             self.walk(lambda c: c.start(), 0, 0)
@@ -159,7 +166,7 @@
             lambda o, l: a_recv.at[k, o * LANES + l],
             lambda o, l, gg: a_core.at[k, o * LANES + l, gg],
             lambda o, l, d: a_send.at[k, o * LANES + l, d],
-            0, line, False)
+            0, line, False, 0 if k % 2 == 0 else line - 1)
 
     lines = group // LANES
 
@@ -321,29 +328,39 @@
         for _ in range(min(count, len(todo))):
             todo.pop(0)()
 
-    def begin(a, h):
-        for j in range(n_width):
-            handed(a, h, j)
-            factors[a][h][j].start()
+    def begin_own(a):
+        for h in range(PARTS):
+            factors[a][h][0].start()
+
+    def begin_rest(a):
+        for h in range(PARTS):
+            for j in range(1, n_width):
+                handed(a, h, j)
+                factors[a][h][j].start()
 
     chunks[0].start()
     for k in range(2 * CUTS):
         chunk = chunks[k]
-        todo = []
+        last = k == 2 * CUTS - 1
+        todo, sums = [], []
         if k > 0:
             todo = [functools.partial(multiply, (k - 1) * BLOCKS + b) for b in range(BLOCKS)]
+        if last:
+            sums = [functools.partial(total, 0, h) for h in range(PARTS)]
         for step in range(1, line):
             chunk.along(step)
             run(todo, 1)
-            if step == line - 1 and k + 1 < 2 * CUTS:
-                chunks[k + 1].start()
+            run(sums, 1)
+            if step == line - 1:
+                if last:
+                    run(sums, len(sums))
+                    begin_own(0)
+                else:
+                    chunks[k + 1].start()
             chunk.across(step - 1)
         run(todo, len(todo))
-        if k == 2 * CUTS - 1:
-            for h in range(PARTS):
-                total(0, h)
-            for h in range(PARTS):
-                begin(0, h)
+        if last:
+            begin_rest(0)
         chunk.across(line - 1)
         chunk.finish()
 
@@ -358,23 +375,20 @@
             for one in factors[a][h]:
                 one.across(line - 1)
 
-    for f in range(CUTS):
-        chunks[f].drain()
-        train_load(0, f).start()
     todo = [functools.partial(multiply, (2 * CUTS - 1) * BLOCKS + b) for b in range(BLOCKS)]
-
-    def second():
+    run(todo, 2)
+
+    def reuse(a):
         for f in range(CUTS):
-            chunks[CUTS + f].drain()
-            train_load(1, f).start()
-
-    todo.append(second)
+            chunks[a * CUTS + f].drain()
+            train_load(a, f).start()
+
+    reuse(0)
+    todo.append(functools.partial(reuse, 1))
+    todo += [functools.partial(total, 1, h) for h in range(PARTS)]
+    todo += [functools.partial(begin_own, 1), functools.partial(begin_rest, 1)]
     spread(0, todo)
     run(todo, len(todo))
-    for h in range(PARTS):
-        total(1, h)
-    for h in range(PARTS):
-        begin(1, h)
     for f in range(CUTS):
         train_load(0, f).wait()
 
@@ -396,10 +410,10 @@
     for h in range(PARTS):
         for one in factors[1][h]:
             one.finish()
-        for c in range(n_width):
-            project(1, h, c)
-    for j in range(1, n_width):
-        p_copy(1, j).start()
+        for j in [*range(1, n_width), 0]:
+            project(1, h, other(j))
+            if h == PARTS - 1 and j > 0:
+                p_copy(1, j).start()
     shares = []
     for a in range(2):
         for j in range(1, n_width):

time: 255 us -> 248 us (0.973); the launches traced: 252 us -> 248 us
  Pallas kernels: 250 us -> 246 us
    pallas_call x1, Pallas kernels: 250 us -> 246 us  [local(): pl.pallas_call(functools.partial(pipeline, n_dp, n_width, n_grid, (scale,...]
where the time goes in v2:
time: 248 us
  Pallas kernels  246 us (99%)
    pallas_call x1, Pallas kernels, local(): pl.pallas_call(functools.partial(pipeline, n_dp, n_width, n_grid, (scale,...  246 us

profile of v2, /device:TPU:0, one launch (start us, length us, event | category | flops | bytes accessed | tf_op | source)
XLA Modules:
  0.0 248.0 jit_solution(7462910213909757649)
XLA Ops:
  0.0 0.0 copy-start.1
  0.0 0.0 copy-start
  0.0 246.4 %shard_map.82 = f32[2,8,384]{2,1,0:T(8,128)} custom-call(bf16[64,8192]{1,0:T(8,128)(2,1)} %qa.1, bf16[64,8192]{1,0:T(8,128)(2,1)} %qg.1, bf16[1024,8192]{1,0:T(8,128)(2,1)} %ia.1, bf16[1024,8192]{1,0:T(8,128)(2,1)} %ig.1, bf16[384,8192]{1,0:T(8,128)(2,1)} %ta.1, bf16[384,8192]{1,0:T(8,128)(2,1)} %tg.1), custom_call_target="tpu_custom_call" | custom-call | flops 23622320128 | bytes 62914560 | tf_op jit(solution)/shard_map/pallas_call | solution.py:475
  246.4 0.0 copy-done.1
  246.4 0.1 broadcast_compare_fusion
  246.5 0.8 select_reduce_fusion
  247.3 0.0 copy-done
  247.3 0.6 multiply_bitcast_fusion
  (2 shorter events, 0.0 us)
Async XLA Ops:
  0.0 246.4 %copy-start.1 = (s32[16]{0:T(128)S(1)}, s32[16]{0:T(128)}, u32[]{:S(2)}) copy-start(s32[16]{0:T(128)} %param.14) | copy-start | bytes 196
  0.0 247.3 %copy-start = (s32[384]{0:T(512)S(1)}, s32[384]{0:T(512)}, u32[]{:S(2)}) copy-start(s32[384]{0:T(512)} %param.15) | copy-start | bytes 4612
